TPU v7x, 512 devices: a whole 4x8x8 slice. The times are simulated.
512 devices in a mesh: row: 32 (over z, x_hi, core), col: 16 (over x_lo, y).
Axes of the slice: x: 4 (x_hi: 2, x_lo: 2; x = x_hi * 2 + x_lo), y: 8, z: 8, core: 2. Of those that a mesh axis runs over, the one named last changes fastest.
Arguments:
- fock_matrix: bfloat16 [12288, 12288], P('row', 'col'), may hold values from -40 to 40, as said below
- density_matrix: bfloat16 [12288, 12288], P('row', 'col'), may hold values from -1.25 to 1.25, as said below
- fock_blocks: int32 [96, 96], replicated, may hold values from 0 to 1, as said below
- density_blocks: int32 [96, 96], replicated, may hold values from 0 to 1, as said below
- slab_offset: int32 [1], replicated, may hold values from 0 to 65535
Outputs:
- commutator: float32 [12288, 12288], P('row', 'col')
Inputs may be any that keep to these rules, and one draw needn't show every extreme that they name: `fock_matrix`: symmetric. `density_matrix`: symmetric. `fock_blocks`: symmetric 0/1 table of occupied blocks; every block on the diagonal is occupied. `density_blocks`: symmetric 0/1 table of occupied blocks; every block on the diagonal is occupied.
All inputs are finite; a program needn't handle non-finite values.
Results may differ from a plain program's by a relative error of at most 0.00035.
Values may be sent and summed in bfloat16 or wider, within the bound.
A program may use at most 64 MiB of HBM per device.

v0:
```python
import functools

import jax
import jax.numpy as jnp
import numpy as np
from jax import lax
from jax.experimental import pallas as pl
from jax.experimental.pallas import tpu as pltpu
from jax.sharding import PartitionSpec as P

BLK = 128
GRID = 16
HALF = 384
TILE = 768
WINDOW = 4
CUTS = 4
PIECE = TILE // CUTS
LOWER = CUTS // 2
HOPS = 6
LAG = 2
STEPS = 6 + 2 * LAG
SWAPPED, OWN = 12, 13
CROSS, LAST = 7, 8
GOT = 14
WIDTH = 256
MESH = pl.DeviceIdType.MESH


def div(a, b):
    return a // b if isinstance(a, int) else lax.div(a, np.int32(b))


def rem(a, b):
    return a % b if isinstance(a, int) else lax.rem(a, np.int32(b))


def where(cond, a, b):
    if isinstance(cond, bool):
        return a if cond else b
    return jnp.where(cond, a, b)


def flag(cond):
    return where(cond, 1, 0)


def at(pair, n):
    return where(n == 0, pair[0], pair[1])


def differ(a, b):
    return a + b - 2 * a * b


class RowRoute:
    def __init__(self, i, y, off):
        t = rem(i + off, GRID)
        base = rem(t + 2, 8) - 2
        flip = rem(div(t + 2, 8), 2)
        first = (
            where(base <= 3, 4, 0),
            where(base == 0, 3, where(base == 1, 2, where(base == 4, 2, flag(base == 5)))),
        )
        self.y = y
        self.flip = (flip, where(base < 0, flip, 1 - flip))
        self.low = (where(base < 0, 0, base), where(base < 0, 1, 5 - base))
        self.swap = where(base <= 0, flip, where(base == 5, 1 - flip, 0))
        self.zero = flag((base <= 0) | (base == 5)) * (1 - self.swap)
        self.zero_s = where(base == 5, 3, where(base < 0, -base, 0))
        self.base, self.far = base, where(base < 0, 0, 8)
        self.start = tuple(
            flag(base < 0) * self.swap * self.first_turned(way) for way in (0, 1)
        )
        self.hops, self.slot = [], []
        for a in first:
            down = where(base < 0, base + 3, where(a > 0, base + a - 1, 0))
            up = where(base < 0, -base, where(a < 4, 8 - base - a, 0))
            self.hops.append((down, up))
            slots = []
            for s in range(4):
                d = base + s
                from_down = where(base < 0, flag(d >= 0), flag(s < a))
                hop = where(from_down == 1, d, where(base < 0, -d, 8 - d))
                turned = where(from_down == 1, self.flip[0], self.flip[1])
                moved = where(from_down == 1, hop - 1, hop + HOPS - 1)
                slots.append(where(hop == 0, OWN - turned, moved))
            self.slot.append(slots)
        self.both = tuple(flag(self.hops[0][w] * self.hops[1][w] > 0) for w in (0, 1))

    def step_of(self, way, h):
        return where(way == 0, h, self.far - h) - self.base

    def first_turned(self, way):
        source = self.y if way == 0 else 7 - self.y
        low = where(self.low[way] > 1, self.low[way], 1)
        return differ(self.flip[way], flag(low > source))

    def crosses(self, way, h):
        source = where(way == 0, rem(self.y + h, 8), 7 - rem(self.y + 8 - h, 8))
        low, flip = at(self.low, way), at(self.flip, way)
        now = differ(flip, flag(where(h > low, h, low) > source))
        new = differ(flip, flag(where(h + 1 > low, h + 1, low) > source))
        return differ(where(h == 0, at(self.start, way), now), new)


class ColRoute:
    def __init__(self, j, x_hi, off):
        t = rem(j + off, GRID)
        odd = rem(t, 2)
        u = rem(div(t + odd, 2), 8)
        self.down = (
            flag(u <= 3),
            where(u <= 1, 1, where(u == 4, 1, where(u == 2, odd, where(u == 5, odd, 0)))),
        )
        self.last_down = (where(u == 3, 1, where(u == 4, 0, 1 - odd)), 1 - odd)
        self.same = flag(self.down[0] == self.down[1])
        self.hops = [where(n == 1, u + 1, 8 - u) for n in self.down]
        self.need = [
            (where(n == 1, u, 8 - u), where(n == 1, u + 1, 7 - u)) for n in self.down
        ]
        self.cross_s = [3 - odd - 2 * last for last in self.last_down]
        self.last_s = [1 - odd + 2 * last for last in self.last_down]
        self.odd = odd
        self.hop_in, self.hop_out, self.slot = [], [], []
        for n, last, need in zip(self.down, self.last_down, self.need):
            w_in = u + x_hi - odd + 1 - last
            w_out = u + 1 - x_hi - odd + 1 - last
            self.hop_in.append(where(n == 1, w_in, 8 - w_in))
            self.hop_out.append(where(n == 1, w_out, 8 - w_out))
            low, high = LAST - last, CROSS + last
            self.slot.append([
                where(odd == 0, need[0], low), where(odd == 1, need[0], low),
                where(odd == 0, need[1], high), where(odd == 1, need[1], high),
            ])


def pick(values, s):
    out = values[-1]
    for n in range(len(values) - 2, -1, -1):
        out = jnp.where(s == n, values[n], out)
    return out


def kernel(
    off, fock_ref, density_ref, out_ref, tiles,
    load_sem, give_send, give_recv, row_send, row_recv, swap_send, swap_recv,
    col_send, col_recv, x_send, x_recv, last_send, last_recv, pair_send, pair_recv,
):
    r, c = lax.axis_index("row"), lax.axis_index("col")
    core, x_hi, z = rem(r, 2), rem(div(r, 2), 2), div(r, 4)
    x_lo, y = div(c, 8), rem(c, 8)
    row, col = RowRoute(div(r, 2), y, off), ColRoute(c, x_hi, off)
    y_next = (rem(y + 7, 8), rem(y + 1, 8))
    z_next = (rem(r + 28, 32), rem(r + 4, 32))
    swap_dev = (r, (1 - x_lo) * 8 + y)
    x_dev = (r + 2 - 4 * x_hi, c)
    pair_dev = (r + 1 - 2 * core, c)
    refs = (fock_ref, density_ref)
    early = (row.start[0] + row.start[1]) > 0
    late = (row.swap == 1) & ((row.start[0] + row.start[1]) == 0)

    home = where(core == 0, OWN, 0)
    away = where(core == 0, 0, OWN)
    mine = pl.ds(pl.multiple_of(core * HALF, HALF), HALF)
    other = pl.ds(pl.multiple_of(HALF - core * HALF, HALF), HALF)

    def load(m):
        return pltpu.make_async_copy(refs[m], tiles.at[m, home, mine], load_sem.at[m, 0])

    def keep(m):
        target = tiles.at[m, GOT + row.zero_s, pl.ds(0, HALF)]
        return pltpu.make_async_copy(refs[m], target, load_sem.at[m, 1])

    def remote(src, dst, send, recv, dev):
        return pltpu.make_async_remote_copy(
            src_ref=src, dst_ref=dst, send_sem=send, recv_sem=recv,
            device_id=dev, device_id_type=MESH,
        )

    def give(m):
        return remote(
            refs[m], tiles.at[m, away, mine], give_send.at[m], give_recv.at[m], pair_dev
        )

    def taken(m):
        return remote(
            refs[m], tiles.at[m, home, other], give_send.at[m], give_recv.at[m], pair_dev
        )

    for m in (0, 1):
        load(m).start()

    @pl.when((core == 1) & (row.zero == 1))
    def _():
        for m in (0, 1):
            keep(m).start()

    greet = [swap_dev, x_dev, pair_dev, (z_next[0], c), (z_next[1], c)]
    greet += [(r, x * 8 + v) for x in (0, 1) for v in y_next]
    barrier = pltpu.get_barrier_semaphore()
    for dev in greet:
        pl.semaphore_signal(barrier, inc=1, device_id=dev, device_id_type=MESH)
    pl.semaphore_wait(barrier, len(greet))

    def part(m, slot, q):
        return tiles.at[m, slot, pl.ds(pl.multiple_of(q * PIECE, PIECE), PIECE)]

    def row_copy(m, way, h, q):
        slot = where(h == 0, OWN - at(row.start, way), h - 1 + way * HOPS)
        dev = (r, differ(x_lo, row.crosses(way, h)) * 8 + at(y_next, way))
        return remote(
            part(m, slot, q), part(m, h + way * HOPS, q),
            row_send.at[m, way, h, q], row_recv.at[m, way, h, q], dev,
        )

    def row_hops(m, way):
        return where(m == 0, at(row.hops[0], way), at(row.hops[1], way))

    def swap_copy(m, q):
        return remote(
            part(m, OWN, q), part(m, SWAPPED, q),
            swap_send.at[m, q], swap_recv.at[m, q], swap_dev,
        )

    def col_copy(m, h, q):
        dev = (where(at(col.down, m) == 1, z_next[0], z_next[1]), c)
        return remote(
            part(m, h, q), part(m, h + 1, q),
            col_send.at[m, h, q], col_recv.at[m, h, q], dev,
        )

    def x_copy(m, q):
        return remote(
            part(m, at(col.hop_out, m), q), part(m, CROSS, q),
            x_send.at[m, q], x_recv.at[m, q], x_dev,
        )

    def last_copy(m, q):
        dev = (where(at(col.last_down, m) == 1, z_next[0], z_next[1]), c)
        return remote(
            part(m, CROSS, q), part(m, LAST, q),
            last_send.at[m, q], last_recv.at[m, q], dev,
        )

    def pair_copy(m, slot, s, q, to):
        return remote(
            part(m, slot, q), part(m, GOT + s, to),
            pair_send.at[m, s, to], pair_recv.at[m, s, to], pair_dev,
        )

    def turn(m, shared, step):
        odd = rem(step, 2)
        hop = where((shared == 1) & (step > 0), div(step + 1 - m, 2), step)
        ours = (shared == 0) | (step == 0) | (odd == 1 - m)
        return hop, ours

    for m in (0, 1):
        give(m).start()

    @pl.loop(0, HALF // 8)
    def _(n):
        out_ref[pl.ds(n * 8, 8)] = jnp.zeros((8, TILE), jnp.float32)

    for m in (0, 1):
        load(m).wait()

    @pl.when(core == 0)
    def _():
        @pl.loop(0, HOPS + 2)
        def _(step):
            @pl.loop(0, 4 * CUTS)
            def _(n):
                q, way, m = div(n, 4), rem(div(n, 2), 2), rem(n, 2)
                h, ours = turn(m, at(row.both, way), step)
                hops = row_hops(m, way)
                live = ours & (h <= hops)

                @pl.when((step == 0) & (n == 4 * LOWER))
                def _():
                    for k in (0, 1):
                        taken(k).wait_recv()

                @pl.when(early & (step == 0) & (way == 0))
                def _():
                    swap_copy(m, q).start()

                @pl.when(live & (h >= 1))
                def _():
                    row_copy(m, way, h - 1, q).wait_recv()

                @pl.when(live & (h < hops) & ((h >= 1) | (at(row.start, way) == 0)))
                def _():
                    row_copy(m, way, h, q).start()

                @pl.when(live & (h >= 1) & (h >= at(row.low, way)) & (q >= LOWER))
                def _():
                    slot = h - 1 + way * HOPS
                    pair_copy(m, slot, row.step_of(way, h), q, q - LOWER).start()

            @pl.when((step == 0) & (row.swap == 1))
            def _():
                @pl.loop(0, 2 * CUTS)
                def _(n):
                    q, m = div(n, 2), rem(n, 2)

                    @pl.when(late)
                    def _():
                        swap_copy(m, q).start()

                    @pl.when(early)
                    def _():
                        swap_copy(m, q).wait_recv()

                        @pl.loop(0, 2)
                        def _(way):
                            @pl.when((at(row.start, way) == 1) & (row_hops(m, way) > 0))
                            def _():
                                row_copy(m, way, 0, q).start()

            @pl.when((step == HOPS + 1) & (row.swap == 1))
            def _():
                @pl.loop(0, 2 * CUTS)
                def _(n):
                    q, m = div(n, 2), rem(n, 2)

                    @pl.when(late)
                    def _():
                        swap_copy(m, q).wait_recv()

                    @pl.when(q >= LOWER)
                    def _():
                        pair_copy(m, SWAPPED, row.zero_s, q, q - LOWER).start()

        @pl.loop(0, WINDOW)
        def _(s):
            @pl.loop(0, 2 * CUTS)
            def _(n):
                q, m = div(n, 2), rem(n, 2)
                pair_copy(m, GOT + s, s, q, q).wait_recv()

    @pl.when(core == 1)
    def _():
        for m in (0, 1):
            taken(m).wait_recv()

        @pl.loop(0, STEPS + 1)
        def _(step):
            @pl.loop(0, 2 * CUTS)
            def _(n):
                q, m = div(n, 2), rem(n, 2)
                h, ours = turn(m, col.same, step)
                hops = at(col.hops, m)
                live = ours & (h <= hops)
                first, second = (where(m == 0, col.need[0][k], col.need[1][k]) for k in (0, 1))
                there = at(col.hop_in, m)
                due = where((col.same == 1) & (there > 0), 2 * there - 1 + m, there)

                @pl.when(live & (h >= 1))
                def _():
                    col_copy(m, h - 1, q).wait_recv()

                @pl.when(live & (h < hops))
                def _():
                    col_copy(m, h, q).start()

                @pl.when(live & (h == at(col.hop_out, m)))
                def _():
                    x_copy(m, q).start()

                @pl.when(live & ((h == first) | (h == second)))
                def _():
                    pair_copy(m, h, col.odd + where(h == second, 2, 0), q, q).start()

                @pl.when(step == due + LAG)
                def _():
                    x_copy(m, q).wait_recv()
                    last_copy(m, q).start()

                @pl.when(step == due + 2 * LAG)
                def _():
                    last_copy(m, q).wait_recv()

                @pl.when((step == due + LAG) | (step == due + 2 * LAG))
                def _():
                    slot = where(step == due + LAG, CROSS, LAST)
                    s = where(step == due + LAG, at(col.cross_s, m), at(col.last_s, m))
                    pair_copy(m, slot, s, q, q).start()

        @pl.loop(0, WINDOW)
        def _(s):
            @pl.when((row.zero == 0) | (s != row.zero_s))
            def _():
                @pl.loop(0, 2 * LOWER)
                def _(n):
                    q, m = div(n, 2), rem(n, 2)
                    pair_copy(m, GOT + s, s, q, q).wait_recv()

        @pl.when(row.zero == 1)
        def _():
            for m in (0, 1):
                keep(m).wait()


    @pl.loop(0, WINDOW)
    def _(s):
        left = [where(core == 0, pick(row.slot[m], s), GOT + s) for m in (0, 1)]
        right = [where(core == 0, GOT + s, pick(col.slot[m], s)) for m in (0, 1)]

        @pl.loop(0, TILE // WIDTH)
        def _(n):
            span = pl.ds(pl.multiple_of(n * WIDTH, WIDTH), WIDTH)
            fp = jnp.dot(
                tiles[0, left[0], :HALF], tiles[1, right[1], :, span],
                preferred_element_type=jnp.float32,
            )
            pf = jnp.dot(
                tiles[1, left[1], :HALF], tiles[0, right[0], :, span],
                preferred_element_type=jnp.float32,
            )
            out_ref[:, span] += fp - pf

    for m in (0, 1):
        give(m).wait_send()

    @pl.loop(0, 2 * CUTS)
    def _(n):
        q, m = div(n, 2), rem(n, 2)

        @pl.when((core == 0) & (row.swap == 1))
        def _():
            swap_copy(m, q).wait_send()

        @pl.when(core == 1)
        def _():
            x_copy(m, q).wait_send()
            last_copy(m, q).wait_send()

        @pl.loop(0, HOPS)
        def _(h):
            @pl.loop(0, 2)
            def _(way):
                @pl.when((core == 0) & (h < row_hops(m, way)))
                def _():
                    row_copy(m, way, h, q).wait_send()

            @pl.when((core == 1) & (h < at(col.hops, m)))
            def _():
                col_copy(m, h, q).wait_send()

        @pl.loop(0, WINDOW)
        def _(s):
            sent = (q < LOWER) & ((row.zero == 0) | (s != row.zero_s))

            @pl.when((core == 1) | sent)
            def _():
                pair_copy(m, GOT + s, s, q, q).wait_send()


def commute(fock, density, off):
    sems = [(2, 2)] + [(2,)] * 2 + [(2, 2, HOPS, CUTS)] * 2 + [(2, CUTS)] * 2
    sems += [(2, HOPS, CUTS)] * 2 + [(2, CUTS)] * 4 + [(2, WINDOW, CUTS)] * 2
    return pl.pallas_call(
        functools.partial(kernel, off),
        out_shape=jax.ShapeDtypeStruct((HALF, TILE), jnp.float32),
        in_specs=[pl.BlockSpec(memory_space=pl.ANY)] * 2,
        out_specs=pl.BlockSpec(memory_space=pltpu.VMEM),
        scratch_shapes=[
            pltpu.VMEM((2, GOT + WINDOW, TILE, TILE), jnp.bfloat16),
        ] + [pltpu.SemaphoreType.DMA(shape) for shape in sems],
        compiler_params=pltpu.CompilerParams(
            collective_id=off, has_side_effects=True, vmem_limit_bytes=52 << 20
        ),
    )(fock, density)


def masked_piece(values, occupied, first_row, first_col):
    row_blocks = values.shape[0] // BLK
    col_blocks = values.shape[1] // BLK
    window = lax.dynamic_slice(occupied, (first_row, first_col), (row_blocks, col_blocks))
    blocks = (
        values.reshape(row_blocks, BLK, col_blocks, BLK)
        * window.astype(values.dtype)[:, None, :, None]
    )
    return blocks.reshape(values.shape)


def shards(fock_matrix, density_matrix, fock_blocks, density_blocks, slab_offset):
    corner = (lax.axis_index("row") * (HALF // BLK), lax.axis_index("col") * (TILE // BLK))
    fock = masked_piece(fock_matrix, fock_blocks, *corner)
    density = masked_piece(density_matrix, density_blocks, *corner)
    fock, density = lax.optimization_barrier((fock, density))
    branches = [functools.partial(commute, off=off) for off in range(GRID)]
    return lax.switch(slab_offset[0] % GRID, branches, fock, density)


def solution(mesh):
    placed = (P("row", "col"), P("row", "col"), P(), P(), P())
    return jax.shard_map(
        shards, mesh=mesh, in_specs=placed, out_specs=P("row", "col"), check_vma=False
    )
```

profile of v0, /device:TPU:388, one launch (start us, length us, event | category | flops | bytes accessed | tf_op | source)
XLA Modules:
  0.0 138.8 jit_solution(10841864326693966880)
XLA Ops:
  0.0 0.0 copy-start
  0.7 0.8 dynamic-slice_convert_fusion
  1.5 0.2 mul.33
  1.7 0.0 copy-done
  1.7 0.0 copy-start.1
  1.7 0.1 bitcast_multiply_fusion
  1.8 0.2 mul.30
  2.0 0.8 copy-done.1
  2.8 0.1 bitcast_multiply_fusion.1
  2.9 134.9 %conditional.1 = (f32[384,768]{1,0:T(8,128)S(1)}) conditional(s32[]{:T(128)} %clamp.3, (bf16[384,768]{1,0:T(8,128)(2,1)S(1)}, bf16[384,768]{1,0:T(8,128)(2,1)S(1)}) %tuple.38, (bf16[384,768]{1,0:T(8,128)(2,1)S(1)}, bf16[384,768]{1,0:T(8,128)(2,1)S(1)}) %tuple.38, (bf16[384,768]{1,0:T(8,128)(2,1)S(1)}, ...), branch_computations={%region_0.1_spmd, %region_1.2_spmd, %region_2.3_spmd, %region_3.4_... | conditional | bytes 8 | solution.py:493
  3.1 134.7 %branch_9_fun.1 = f32[384,768]{1,0:T(8,128)S(1)} custom-call(bf16[384,768]{1,0:T(8,128)(2,1)S(1)} %get-tuple-element.104.fock_ref, bf16[384,768]{1,0:T(8,128)(2,1)S(1)} %get-tuple-element.105.density_ref), custom_call_target="tpu_custom_call" | custom-call | tf_op jit(solution)/shard_map/cond/branch_9_fun/pallas_call | solution.py:462
  137.8 1.0 copy.44
Async XLA Ops:
  0.0 1.7 %copy-start = (bf16[384,768]{1,0:T(8,128)(2,1)S(1)}, bf16[384,768]{1,0:T(8,128)(2,1)}, u32[]{:S(2)}) copy-start(bf16[384,768]{1,0:T(8,128)(2,1)} %param.22) | copy-start | bytes 1769476
  1.7 1.1 copy-start.1
where the time goes:
time: 139 us
  Pallas kernels  135 us (97%)
  local copies, waits for them, and re-layouts  2.16 us (2%)
    pallas_call x1, Pallas kernels, commute(): pl.pallas_call(functools.partial(kernel, off), out_shape=jax.ShapeDtypeSt...  135 us

commit v1 on v0

--- a/solution.py
+++ b/solution.py
@@ -17,8 +17,8 @@
 PIECE = TILE // CUTS
 LOWER = CUTS // 2
 HOPS = 6
-LAG = 2
-STEPS = 6 + 2 * LAG
+LAG = 3
+STEPS = HOPS + LAG
 SWAPPED, OWN = 12, 13
 CROSS, LAST = 7, 8
 GOT = 14
@@ -59,7 +59,7 @@
         flip = rem(div(t + 2, 8), 2)
         first = (
             where(base <= 3, 4, 0),
-            where(base == 0, 3, where(base == 1, 2, where(base == 4, 2, flag(base == 5)))),
+            where(base == 0, 2, where(base == 1, 1, where(base == 4, 3, 2 * flag(base == 5)))),
         )
         self.y = y
         self.flip = (flip, where(base < 0, flip, 1 - flip))
@@ -331,23 +331,19 @@
                     def _():
                         pair_copy(m, SWAPPED, row.zero_s, q, q - LOWER).start()
 
-        @pl.loop(0, WINDOW)
-        def _(s):
-            @pl.loop(0, 2 * CUTS)
-            def _(n):
-                q, m = div(n, 2), rem(n, 2)
-                pair_copy(m, GOT + s, s, q, q).wait_recv()
-
     @pl.when(core == 1)
     def _():
-        for m in (0, 1):
-            taken(m).wait_recv()
-
         @pl.loop(0, STEPS + 1)
         def _(step):
             @pl.loop(0, 2 * CUTS)
             def _(n):
-                q, m = div(n, 2), rem(n, 2)
+                q, m = rem(div(n, 2) + LOWER, CUTS), rem(n, 2)
+
+                @pl.when((step == 0) & (n == 2 * LOWER))
+                def _():
+                    for k in (0, 1):
+                        taken(k).wait_recv()
+
                 h, ours = turn(m, col.same, step)
                 hops = at(col.hops, m)
                 live = ours & (h <= hops)
@@ -375,34 +371,37 @@
                 def _():
                     x_copy(m, q).wait_recv()
                     last_copy(m, q).start()
-
-                @pl.when(step == due + 2 * LAG)
-                def _():
-                    last_copy(m, q).wait_recv()
-
-                @pl.when((step == due + LAG) | (step == due + 2 * LAG))
-                def _():
-                    slot = where(step == due + LAG, CROSS, LAST)
-                    s = where(step == due + LAG, at(col.cross_s, m), at(col.last_s, m))
-                    pair_copy(m, slot, s, q, q).start()
-
-        @pl.loop(0, WINDOW)
-        def _(s):
-            @pl.when((row.zero == 0) | (s != row.zero_s))
-            def _():
-                @pl.loop(0, 2 * LOWER)
-                def _(n):
-                    q, m = div(n, 2), rem(n, 2)
-                    pair_copy(m, GOT + s, s, q, q).wait_recv()
-
-        @pl.when(row.zero == 1)
+                    pair_copy(m, CROSS, at(col.cross_s, m), q, q).start()
+
+    order = (col.odd, col.odd + 2, col.cross_s[1], col.last_s[1])
+
+    @pl.loop(0, WINDOW)
+    def _(k):
+        s = pick(order, k)
+
+        @pl.when((core == 1) & (k == 2))
+        def _():
+            @pl.loop(0, 2 * CUTS)
+            def _(n):
+                q, m = rem(div(n, 2) + LOWER, CUTS), rem(n, 2)
+                last_copy(m, q).wait_recv()
+                pair_copy(m, LAST, at(col.last_s, m), q, q).start()
+
+        kept = (core == 1) & (row.zero == 1) & (s == row.zero_s)
+
+        @pl.when(kept)
         def _():
             for m in (0, 1):
                 keep(m).wait()
 
-
-    @pl.loop(0, WINDOW)
-    def _(s):
+        @pl.loop(0, 2 * CUTS)
+        def _(n):
+            q, m = div(n, 2), rem(n, 2)
+
+            @pl.when((core == 0) | ((q < LOWER) & jnp.logical_not(kept)))
+            def _():
+                pair_copy(m, GOT + s, s, q, q).wait_recv()
+
         left = [where(core == 0, pick(row.slot[m], s), GOT + s) for m in (0, 1)]
         right = [where(core == 0, GOT + s, pick(col.slot[m], s)) for m in (0, 1)]
 

time: 139 us -> 130 us (0.935)
  the two profiles are of different devices: /device:TPU:388 before, /device:TPU:258 now
where the time goes in v1:
time: 130 us
  Pallas kernels  125 us (96%)
  local copies, waits for them, and re-layouts  2.16 us (2%)
    pallas_call x1, Pallas kernels, commute(): pl.pallas_call(functools.partial(kernel, off), out_shape=jax.ShapeDtypeSt...  125 us

profile of v1, /device:TPU:258, one launch (start us, length us, event | category | flops | bytes accessed | tf_op | source)
XLA Modules:
  0.0 129.7 jit_solution(14451343164329872968)
XLA Ops:
  0.0 0.0 copy-start
  0.7 0.8 dynamic-slice_convert_fusion
  1.5 0.2 mul.33
  1.7 0.0 copy-done
  1.7 0.0 copy-start.1
  1.7 0.1 bitcast_multiply_fusion
  1.8 0.2 mul.30
  2.0 0.8 copy-done.1
  2.8 0.1 bitcast_multiply_fusion.1
  2.9 125.8 %conditional.1 = (f32[384,768]{1,0:T(8,128)S(1)}) conditional(s32[]{:T(128)} %clamp.3, (bf16[384,768]{1,0:T(8,128)(2,1)S(1)}, bf16[384,768]{1,0:T(8,128)(2,1)S(1)}) %tuple.38, (bf16[384,768]{1,0:T(8,128)(2,1)S(1)}, bf16[384,768]{1,0:T(8,128)(2,1)S(1)}) %tuple.38, (bf16[384,768]{1,0:T(8,128)(2,1)S(1)}, ...), branch_computations={%region_0.1_spmd, %region_1.2_spmd, %region_2.3_spmd, %region_3.4_... | conditional | bytes 8 | solution.py:492
  2.9 125.5 %branch_0_fun.1 = f32[384,768]{1,0:T(8,128)S(1)} custom-call(bf16[384,768]{1,0:T(8,128)(2,1)S(1)} %get-tuple-element.72.fock_ref, bf16[384,768]{1,0:T(8,128)(2,1)S(1)} %get-tuple-element.73.density_ref), custom_call_target="tpu_custom_call" | custom-call | tf_op jit(solution)/shard_map/cond/branch_0_fun/pallas_call | solution.py:461
  128.6 1.0 copy.44
Async XLA Ops:
  0.0 1.7 %copy-start = (bf16[384,768]{1,0:T(8,128)(2,1)S(1)}, bf16[384,768]{1,0:T(8,128)(2,1)}, u32[]{:S(2)}) copy-start(bf16[384,768]{1,0:T(8,128)(2,1)} %param.22) | copy-start | bytes 1769476
  1.7 1.1 copy-start.1
